TPU v7x, 32 devices: a whole 2x2x4 slice. The times are simulated.
32 devices in a mesh: grp: 2 (over y), side: 2 (over core), shard: 8 (over z, x).
Axes of the slice: x: 2, y: 2, z: 4, core: 2. Of those that a mesh axis runs over, the one named last changes fastest.
Arguments:
- queries: bfloat16 [256, 3072], P(('grp', 'shard')), parts along dimension 0, may hold values from -100 to 100
- cache_keys: bfloat16 [256, 128, 512], P(('grp', 'shard')), parts along dimension 0, may hold values from -3 to 3
- cache_values: bfloat16 [256, 128, 512], P(('grp', 'shard')), parts along dimension 0, may hold values from -4 to 4
- lengths: int32 [256], P(('grp', 'shard')), parts along dimension 0, may hold values from 32 to 128
- residual_in: bfloat16 [256, 3072], P(('grp', 'shard')), parts along dimension 0, may hold values from -6 to 6
- norm_gain: float32 [3072], replicated, may hold values from 0.1 to 1.9
- expert_ids: int32 [256, 2], P(('grp', 'shard')), parts along dimension 0, may hold values from 0 to 3, all different within a row; in each aligned block of 16 rows (0 to 15, 16 to 31, ...) at most 12 rows name the same one
- gate_values: bfloat16 [256, 2], P(('grp', 'shard')), parts along dimension 0, may hold values from 0.19921875 to 1
- w_gate: bfloat16 [3072, 4096], P(None, 'shard'), may hold values from -0.109375 to 0.109375
- w_up: bfloat16 [3072, 4096], P(None, 'shard'), may hold values from -0.109375 to 0.109375
- w_down: bfloat16 [4096, 3072], P('shard'), may hold values from -0.1875 to 0.1875
Outputs:
- mixed: bfloat16 [256, 3072], P(('grp', 'shard'), 'side'), parts along dimension 0
There are 2 independent parts, one for each index of `grp`. A program takes and returns all parts, laid end to end along the dimension named above; an argument that names none is the same for every part. Nothing has to cross between parts.
Inputs may be any that keep to these rules, and one draw needn't show every extreme that they name: `expert_ids`: the 2 experts of a row differ. Among the 16 rows of one device no expert is named by more than 12 rows, a bound that some block reaches.
All inputs are finite; a program needn't handle non-finite values.
Results may differ from a plain program's by a relative error of at most 0.0061.
Values may be sent and summed in bfloat16 or wider, within the bound.
A program may use at most 128 MiB of HBM per device.

v0:
```python
import math

import jax
import jax.numpy as jnp
from jax import lax
from jax.sharding import PartitionSpec as P

HD = 128
QH = 24
KVH = 4
EXPERTS = 4
MOST = 12


def attend(queries, cache_keys, cache_values, lengths):
    row_count = cache_keys.shape[0]
    context = cache_keys.shape[1]
    query_heads = queries.reshape(row_count, KVH, QH // KVH, HD)
    key_heads = cache_keys.reshape(row_count, context, KVH, HD)
    value_heads = cache_values.reshape(row_count, context, KVH, HD)
    scores = jnp.einsum(
        "rkgd,rckd->rkgc", query_heads, key_heads, preferred_element_type=jnp.float32
    ) / math.sqrt(HD)
    visible = jnp.arange(context)[None, None, None, :] < lengths[:, None, None, None]
    scores = jnp.where(visible, scores, -1e30)
    peak_score = jnp.max(scores, axis=-1, keepdims=True)
    weights = jnp.exp(scores - peak_score)
    probability = (weights / jnp.sum(weights, axis=-1, keepdims=True)).astype(jnp.bfloat16)
    mixed = jnp.einsum(
        "rkgc,rckd->rkgd", probability, value_heads, preferred_element_type=jnp.float32
    )
    return mixed.reshape(row_count, QH * HD)


def normalize(resid, norm_gain):
    widened = resid.astype(jnp.float32)
    scale = lax.rsqrt(jnp.mean(widened * widened, axis=-1, keepdims=True) + 1e-05)
    return (widened * scale * norm_gain).astype(jnp.bfloat16)


def route_tables(id_table, gate_table, expert_list):
    match = id_table[None] == expert_list[:, None, None, None]
    hit_count = jnp.sum(match.astype(jnp.int32), axis=-1)
    ranked = jnp.cumsum(hit_count, axis=-1) - hit_count
    slot_index = jnp.arange(MOST)
    chosen = (hit_count[:, :, None, :] > 0) & (
        ranked[:, :, None, :] == slot_index[None, None, :, None]
    )
    row_gate = jnp.sum(jnp.where(match, gate_table.astype(jnp.float32)[None], 0.0), axis=-1)
    slot_gate = jnp.sum(jnp.where(chosen, row_gate[:, :, None, :], 0.0), axis=-1)
    return (chosen, slot_gate)


def expert_part(block_in, w_gate, w_up, w_down):
    gate_pre = jnp.dot(block_in, w_gate, preferred_element_type=jnp.float32)
    up_pre = jnp.dot(block_in, w_up, preferred_element_type=jnp.float32)
    hidden = (jax.nn.silu(gate_pre) * up_pre).astype(jnp.bfloat16)
    return jnp.dot(hidden, w_down, preferred_element_type=jnp.float32)


def body(
    queries,
    cache_keys,
    cache_values,
    lengths,
    residual_in,
    norm_gain,
    expert_ids,
    gate_values,
    w_gate,
    w_up,
    w_down,
):
    row_count, model_width = residual_in.shape
    choose_count = expert_ids.shape[1]
    shards = lax.axis_size("shard")
    group_size = shards // EXPERTS
    expert = lax.axis_index("shard") // group_size
    row_index = jnp.arange(row_count)
    attended = attend(queries, cache_keys, cache_values, lengths)
    resid = (residual_in.astype(jnp.float32) + attended).astype(jnp.bfloat16)
    all_rows, all_ids, all_gates = (
        lax.all_gather(resid, "shard", axis=0, tiled=True),
        lax.all_gather(expert_ids, "shard", axis=0, tiled=True),
        lax.all_gather(gate_values, "shard", axis=0, tiled=True),
    )
    normed = normalize(all_rows, norm_gain).reshape(shards, row_count, model_width)
    chosen, slot_gate = route_tables(
        all_ids.reshape(shards, row_count, choose_count),
        all_gates.reshape(shards, row_count, choose_count),
        jnp.reshape(expert, (1,)),
    )
    chosen = chosen[0]
    block_in = jnp.einsum(
        "smr,srd->smd", chosen.astype(jnp.bfloat16), normed, preferred_element_type=jnp.float32
    ).astype(jnp.bfloat16)
    partial_value = expert_part(block_in.reshape(-1, model_width), w_gate, w_up, w_down).reshape(
        shards, MOST, model_width
    )
    weighted = partial_value * slot_gate[0][..., None]
    slot_row = jnp.sum(jnp.where(chosen, row_index[None, None, :], 0), axis=-1)
    owner = (slot_row[..., None] == row_index[None, None, :]).astype(jnp.float32)
    count = lax.axis_size("shard") * row_count
    gathered_back = jnp.einsum("smr,smd->srd", owner, weighted, precision=lax.Precision.HIGHEST)
    expert_sum = lax.psum_scatter(
        gathered_back.reshape(count, model_width), "shard", scatter_dimension=0, tiled=True
    )
    mixed = (resid.astype(jnp.float32) + expert_sum).astype(jnp.bfloat16)
    half_width = model_width // 2
    return lax.dynamic_slice_in_dim(mixed, lax.axis_index("side") * half_width, half_width, 1)


def solution(mesh):
    placed = (
        P(("grp", "shard"), None),
        P(("grp", "shard"), None, None),
        P(("grp", "shard"), None, None),
        P(("grp", "shard")),
        P(("grp", "shard"), None),
        P(),
        P(("grp", "shard"), None),
        P(("grp", "shard"), None),
        P(None, "shard"),
        P(None, "shard"),
        P("shard", None),
    )
    return jax.shard_map(
        body, mesh=mesh, in_specs=placed, out_specs=P(("grp", "shard"), "side"), check_vma=False
    )
```

profile of v0, /device:TPU:0, one launch (start us, length us, event | category | flops | bytes accessed | tf_op | source)
XLA Modules:
  0.0 177.6 jit_solution(14500434718492070784)
XLA Ops:
  6.5 0.0 copy-start
  6.5 0.0 reduce-scatter.2.cloned.1.call-start
  6.5 22.6 %all-gather = s32[8,16,2]{1,2,0:T(2,128)S(1)} all-gather(s32[1,16,2]{1,2,0:T(2,128)} %bitcast.33), channel_id=1, replica_groups=mesh['grp'=2,'side'=2,'shard'=8] {'shard'}, dimensions={0}, use_global_device_ids=true | all-gather | bytes 1152 | tf_op jit(solution)/shard_map/all_gather | solution.py:84
  29.2 0.2 reduce_window_sum.11
  29.3 1.3 iota_compare_fusion.4
  30.7 16.4 %all-gather.1 = bf16[8,16,2]{1,2,0:T(2,128)(2,1)S(1)} all-gather(bf16[1,16,2]{1,2,0:T(2,128)(2,1)} %bitcast.34), channel_id=1, replica_groups=mesh['grp'=2,'side'=2,'shard'=8] {'shard'}, dimensions={0}, use_global_device_ids=true | all-gather | bytes 576 | tf_op jit(solution)/shard_map/all_gather | solution.py:85
  47.1 0.2 select_reduce_fusion
  47.3 0.1 select_reduce_fusion.1
  47.4 0.1 copy.20
  47.5 1.0 reshape.121
  48.5 2.8 %fusion.16 = f32[16,4,6,128]{3,2,1,0:T(8,128)S(1)} fusion(bf16[16,4,6,128]{3,2,1,0:T(8,128)(2,1)S(1)} %reshape.121, pred[16,128]{1,0:T(8,128)(4,1)} %iota_compare_fusion.4, bf16[16,128,512]{2,1,0:T(8,128)(2,1)} %param.12), kind=kOutput, calls=%fused_computation.17 | convolution fusion | flops 12681216 | bytes 2394112 | tf_op jit(solution)/shard_map/rkgd,rckd->rkgc/dot_general | solution.py:21
  51.3 0.0 copy-start.1
  51.3 0.3 fusion.38
  51.6 3.2 %fusion.1 = f32[16,4,6,128]{3,2,1,0:T(8,128)} fusion(f32[16,4,6]{2,1,0:T(4,128)S(1)} %fusion.38, f32[16,4,6,128]{3,2,1,0:T(8,128)S(1)} %fusion.16, bf16[16,128,512]{2,1,0:T(8,128)(2,1)} %param.13), kind=kOutput, calls=%fused_computation.2 | convolution fusion | flops 12730879 | bytes 2491904 | tf_op jit(solution)/shard_map/rkgc,rckd->rkgd/dot_general | solution.py:29
  54.8 1.0 reshape.124
  55.8 0.0 copy-done.1
  55.8 32.1 %all_gather.10 = bf16[128,3072]{1,0:T(8,128)(2,1)S(1)} all-gather(bf16[16,3072]{1,0:T(8,128)(2,1)S(1)} %add_convert_fusion), channel_id=1, replica_groups=mesh['grp'=2,'side'=2,'shard'=8] {'shard'}, dimensions={0}, use_global_device_ids=true | all-gather | bytes 884736 | tf_op jit(solution)/shard_map/all_gather | solution.py:83
  87.9 0.2 fusion.7
  88.1 1.0 fusion.9
  89.1 1.2 convolution_convert_fusion
  90.3 2.1 %reshape.126 = bf16[96,3072]{1,0:T(8,128)(2,1)} reshape(bf16[8,12,3072]{2,1,0:T(8,128)(2,1)} %convolution_convert_fusion) | data formatting | bytes 1179648 | tf_op jit(solution)/shard_map/reshape | solution.py:97
  92.4 2.7 %fusion.39 = f32[96,512]{1,0:T(8,128)S(1)} fusion(bf16[96,3072]{1,0:T(8,128)(2,1)} %reshape.126, bf16[3072,512]{1,0:T(8,128)(2,1)} %param.19), kind=kOutput, calls=%fused_computation.52 | convolution fusion | flops 301989888 | bytes 3932160 | tf_op jit(solution)/shard_map/dot_general | solution.py:55
  95.1 0.0 copy-done
  95.1 4.3 %fusion.21 = f32[96,3072]{1,0:T(8,128)} fusion(bf16[512,3072]{1,0:T(8,128)(2,1)S(1)} %copy-done, bf16[96,3072]{1,0:T(8,128)(2,1)} %reshape.126, bf16[3072,512]{1,0:T(8,128)(2,1)} %param.20, f32[96,512]{1,0:T(8,128)S(1)} %fusion.39), kind=kOutput, calls=%fused_computation.21 | convolution fusion | flops 604274688 | bytes 8257536 | tf_op jit(solution)/shard_map/dot_general | solution.py:58
  99.5 2.5 %reshape.127 = f32[8,12,3072]{2,1,0:T(8,128)} reshape(f32[96,3072]{1,0:T(8,128)} %fusion.21) | data formatting | bytes 2359296 | tf_op jit(solution)/shard_map/reshape | solution.py:97
  102.0 3.5 %fusion.10 = f32[8,16,3072]{2,1,0:T(8,128)} fusion(f32[8,12,3072]{2,1,0:T(8,128)} %reshape.127, f32[8,12]{1,0:T(8,128)S(1)} %copy.20, s32[8,12]{1,0:T(8,128)S(1)} %select_reduce_fusion), kind=kOutput, calls=%fused_computation.13 | convolution fusion | flops 56919552 | bytes 2753280 | tf_op jit(solution)/shard_map/smr,smd->srd/dot_general | solution.py:104
  105.6 0.0 reduce-scatter.2.cloned.1.call-update
  105.6 63.6 %reduce-scatter.2.cloned.1.call-done = f32[16,3072]{1,0:T(8,128)} async-done(((f32[128,3072]{1,0:T(8,128)}), f32[16,3072]{1,0:T(8,128)}) %reduce-scatter.2.cloned.1.call-update) | async-done | bytes 196624 | tf_op jit(solution)/shard_map/reduce_scatter | solution.py:105
  169.2 1.5 fusion.29
  (6 shorter events, 0.1 us)
Async XLA Ops:
  6.5 88.6 %copy-start = (bf16[512,3072]{1,0:T(8,128)(2,1)S(1)}, bf16[512,3072]{1,0:T(8,128)(2,1)}, u32[]{:S(2)}) copy-start(bf16[512,3072]{1,0:T(8,128)(2,1)} %param.21) | copy-start | bytes 9437188
  6.5 162.7 %reduce-scatter.2.cloned.1.call-start = ((), (), s32[]{:S(2)}) async-start(), calls=%async_computation.1 | async-start | bytes 1769472 | tf_op jit(solution)/shard_map/reduce_scatter | solution.py:105
  51.3 4.5 %copy-start.1 = (bf16[16,3072]{1,0:T(8,128)(2,1)S(1)}, bf16[16,3072]{1,0:T(8,128)(2,1)}, u32[]{:S(2)}) copy-start(bf16[16,3072]{1,0:T(8,128)(2,1)} %param.15) | copy-start | bytes 294916
Sparse Core Ops, SparseCore 0:
  105.7 63.4 reduce-scatter.1
where the time goes:
time: 178 us
  blocking collectives  71.1 us (40%)
  waiting for transfers between devices  63.6 us (36%)
  matrix products  17.8 us (10%)
  between operations  13.5 us (8%)
  local copies, waits for them, and re-layouts  6.75 us (4%)
  other arithmetic  4.87 us (3%)
    reduce_scatter x1, waiting for transfers between devices, body(): lax.psum_scatter(gathered_back.reshape(count, model_width), 'shard', scat...  63.6 us
    all_gather x1, blocking collectives, body(): lax.all_gather(resid, 'shard', axis=0, tiled=True)  32.1 us
    all_gather x1, blocking collectives, body(): lax.all_gather(expert_ids, 'shard', axis=0, tiled=True)  22.6 us
    all_gather x1, blocking collectives, body(): lax.all_gather(gate_values, 'shard', axis=0, tiled=True)  16.4 us
    dot_general x1, matrix products, expert_part(): return jnp.dot(hidden, w_down, preferred_element_type=jnp.float32)  4.33 us
  transfers between devices with their start and end apart: 1, of which 1 were waited for; matrix products, arithmetic and copies ran while one was open for 0% of the time, Pallas kernels for 0%

commit v1 on v0

v1 whole, which is shorter than its diff:
```python
import functools
import math

import jax
import jax.numpy as jnp
from jax import lax
from jax.experimental import pallas as pl
from jax.experimental.pallas import tpu as pltpu
from jax.sharding import PartitionSpec as P

HD = 128
QH = 24
KVH = 4
EXPERTS = 4
MESH = pl.DeviceIdType.MESH


def kernel(
    n,
    lengths,
    queries,
    cache_keys,
    cache_values,
    residual_in,
    norm_gain,
    expert_ids,
    gate_values,
    w_gate,
    w_up,
    w_down,
    out,
    keys,
    values,
    gate_w,
    up_w,
    down_w,
    heads,
    attended,
    resid_halves,
    rows_in,
    parts,
    returned,
    load_sem,
    row_send,
    row_recv,
    side_send,
    side_recv,
    part_send,
    part_recv,
):
    me = lax.axis_index("shard")
    side = lax.axis_index("side")
    other = 1 - side
    row_count, width = residual_in.shape
    half = width // 2
    context = keys.shape[1]
    group_size = n // EXPERTS

    loads = [
        pltpu.make_async_copy(cache_keys, keys, load_sem.at[0]),
        pltpu.make_async_copy(cache_values, values, load_sem.at[1]),
        pltpu.make_async_copy(w_gate, gate_w, load_sem.at[2]),
        pltpu.make_async_copy(w_up, up_w, load_sem.at[3]),
        pltpu.make_async_copy(
            w_down.at[:, pl.ds(pl.multiple_of(side * half, half), half)], down_w, load_sem.at[4]
        ),
    ]
    for load in loads:
        load.start()

    barrier = pltpu.get_barrier_semaphore()
    pl.semaphore_signal(barrier, inc=1, device_id={"side": other}, device_id_type=MESH)

    def greet(k, carry):
        pl.semaphore_signal(
            barrier, inc=1, device_id={"shard": lax.rem(me + k, n)}, device_id_type=MESH
        )
        return carry

    lax.fori_loop(1, n, greet, 0)

    for h in range(QH):
        heads[:, h, :] = queries[:, h * HD : (h + 1) * HD].astype(jnp.float32)
    group_of = lax.broadcasted_iota(jnp.int32, (QH, HD), 0) // (QH // KVH)
    position = lax.broadcasted_iota(jnp.int32, (QH, context), 1)
    loads[0].wait()
    probabilities = []
    for r in range(row_count):
        q = heads[r]
        spread = jnp.concatenate(
            [jnp.where(group_of == g, q, 0.0) for g in range(KVH)], axis=1
        ).astype(jnp.bfloat16)
        scores = lax.dot_general(
            spread, keys[r], (((1,), (1,)), ((), ())), preferred_element_type=jnp.float32
        ) * (1.0 / math.sqrt(HD))
        scores = jnp.where(position < lengths[r], scores, -1e30)
        weights = jnp.exp(scores - jnp.max(scores, axis=-1, keepdims=True))
        total = jnp.sum(weights, axis=-1, keepdims=True)
        probabilities.append((weights / total).astype(jnp.bfloat16))
    loads[1].wait()
    for r in range(row_count):
        mixed = jnp.dot(probabilities[r], values[r], preferred_element_type=jnp.float32)
        picked = jnp.where(group_of == 0, mixed[:, :HD], 0.0)
        for g in range(1, KVH):
            picked = jnp.where(group_of == g, mixed[:, g * HD : (g + 1) * HD], picked)
        attended[r] = picked

    squares = jnp.zeros((row_count, HD), jnp.float32)
    widened = []
    for h in range(QH):
        cols = slice(h * HD, (h + 1) * HD)
        resid = (residual_in[:, cols].astype(jnp.float32) + attended[:, h, :]).astype(jnp.bfloat16)
        resid_halves[h // (QH // 2), :, (h % (QH // 2)) * HD : (h % (QH // 2) + 1) * HD] = resid
        wide = resid.astype(jnp.float32)
        widened.append(wide)
        squares += wide * wide
    scale = lax.rsqrt(jnp.sum(squares, axis=-1, keepdims=True) * (1.0 / width) + 1e-05)
    for h in range(QH):
        normed = (widened[h] * scale * norm_gain[:, h * HD : (h + 1) * HD]).astype(jnp.bfloat16)
        rows_in[h // (QH // 2), me, :, (h % (QH // 2)) * HD : (h % (QH // 2) + 1) * HD] = normed

    pl.semaphore_wait(barrier, n)

    def row_copy(k):
        return pltpu.make_async_remote_copy(
            src_ref=rows_in.at[side, me],
            dst_ref=rows_in.at[side, me],
            send_sem=row_send.at[k],
            recv_sem=row_recv.at[k],
            device_id={"shard": lax.rem(me + k, n)},
            device_id_type=MESH,
        )

    def side_copy(k):
        source = lax.rem(me - k + n, n)
        return pltpu.make_async_remote_copy(
            src_ref=rows_in.at[side, source],
            dst_ref=rows_in.at[side, source],
            send_sem=side_send.at[k],
            recv_sem=side_recv.at[k],
            device_id={"side": other},
            device_id_type=MESH,
        )

    def part_copy(k):
        target = lax.rem(me + k, n)
        return pltpu.make_async_remote_copy(
            src_ref=parts.at[target],
            dst_ref=returned.at[k],
            send_sem=part_send.at[k],
            recv_sem=part_recv.at[k],
            device_id={"shard": target},
            device_id_type=MESH,
        )

    def each(step):
        def run(k, carry):
            step(k)
            return carry

        lax.fori_loop(1, n, run, 0)

    each(lambda k: row_copy(k).start())

    def pass_on(k):
        row_copy(k).wait_recv()
        side_copy(k).start()

    each(pass_on)
    loads[2].wait()
    loads[3].wait()
    own = rows_in[side].reshape(n * row_count, half)
    own_cols = pl.ds(pl.multiple_of(side * half, half), half)
    gate_pre = jnp.dot(own, gate_w[own_cols, :], preferred_element_type=jnp.float32)
    up_pre = jnp.dot(own, up_w[own_cols, :], preferred_element_type=jnp.float32)
    each(lambda k: side_copy(k).wait_recv())
    swapped = rows_in[other].reshape(n * row_count, half)
    other_cols = pl.ds(pl.multiple_of(other * half, half), half)
    gate_pre += jnp.dot(swapped, gate_w[other_cols, :], preferred_element_type=jnp.float32)
    up_pre += jnp.dot(swapped, up_w[other_cols, :], preferred_element_type=jnp.float32)
    hidden = (gate_pre / (1.0 + jnp.exp(-gate_pre)) * up_pre).astype(jnp.bfloat16)
    loads[4].wait()
    parts[...] = (
        jnp.dot(hidden, down_w[...], preferred_element_type=jnp.float32)
        .astype(jnp.bfloat16)
        .reshape(n, row_count, half)
    )
    each(lambda k: part_copy(k).start())

    ids = expert_ids[...]
    gates = gate_values[...].astype(jnp.float32)

    def weight(source):
        match = ids == lax.div(source, group_size)
        return jnp.sum(jnp.where(match, gates, 0.0), axis=-1, keepdims=True)

    total = weight(me) * parts[me].astype(jnp.float32)

    def gather(k, total):
        part_copy(k).wait_recv()
        return total + weight(lax.rem(me - k + n, n)) * returned[k].astype(jnp.float32)

    total = lax.fori_loop(1, n, gather, total)
    out[...] = (resid_halves[side].astype(jnp.float32) + total).astype(jnp.bfloat16)

    def finish(k):
        row_copy(k).wait_send()
        side_copy(k).wait_send()
        part_copy(k).wait_send()

    each(finish)


def body(
    queries,
    cache_keys,
    cache_values,
    lengths,
    residual_in,
    norm_gain,
    expert_ids,
    gate_values,
    w_gate,
    w_up,
    w_down,
):
    row_count, width = residual_in.shape
    n = lax.axis_size("shard")
    half = width // 2
    hidden = w_down.shape[0]
    vmem = pl.BlockSpec(memory_space=pltpu.VMEM)
    smem = pl.BlockSpec(memory_space=pltpu.SMEM)
    anywhere = pl.BlockSpec(memory_space=pl.ANY)
    dma = pltpu.SemaphoreType.DMA
    return pl.pallas_call(
        functools.partial(kernel, n),
        out_shape=jax.ShapeDtypeStruct((row_count, half), jnp.bfloat16),
        in_specs=[smem, vmem, anywhere, anywhere, vmem, vmem, vmem, vmem, anywhere, anywhere, anywhere],
        out_specs=vmem,
        scratch_shapes=[
            pltpu.VMEM(cache_keys.shape, jnp.bfloat16),
            pltpu.VMEM(cache_values.shape, jnp.bfloat16),
            pltpu.VMEM(w_gate.shape, jnp.bfloat16),
            pltpu.VMEM(w_up.shape, jnp.bfloat16),
            pltpu.VMEM((hidden, half), jnp.bfloat16),
            pltpu.VMEM((row_count, QH, HD), jnp.float32),
            pltpu.VMEM((row_count, QH, HD), jnp.float32),
            pltpu.VMEM((2, row_count, half), jnp.bfloat16),
            pltpu.VMEM((2, n, row_count, half), jnp.bfloat16),
            pltpu.VMEM((n, row_count, half), jnp.bfloat16),
            pltpu.VMEM((n, row_count, half), jnp.bfloat16),
            dma((5,)),
            dma((n,)),
            dma((n,)),
            dma((n,)),
            dma((n,)),
            dma((n,)),
            dma((n,)),
        ],
        compiler_params=pltpu.CompilerParams(
            collective_id=0, has_side_effects=True, vmem_limit_bytes=56 * 1024 * 1024
        ),
    )(
        lengths,
        queries,
        cache_keys,
        cache_values,
        residual_in,
        norm_gain.reshape(1, width),
        expert_ids,
        gate_values,
        w_gate,
        w_up,
        w_down,
    )


def solution(mesh):
    placed = (
        P(("grp", "shard"), None),
        P(("grp", "shard"), None, None),
        P(("grp", "shard"), None, None),
        P(("grp", "shard")),
        P(("grp", "shard"), None),
        P(),
        P(("grp", "shard"), None),
        P(("grp", "shard"), None),
        P(None, "shard"),
        P(None, "shard"),
        P("shard", None),
    )
    return jax.shard_map(
        body, mesh=mesh, in_specs=placed, out_specs=P(("grp", "shard"), "side"), check_vma=False
    )
```

time: 178 us -> 33 us (0.19)
  the two profiles are of different devices: /device:TPU:0 before, /device:TPU:25 now
where the time goes in v1:
time: 33 us; the launch traced here: 32.7 us
  Pallas kernels  28.6 us (87%)
  local copies, waits for them, and re-layouts  4.1 us (12%)
    pallas_call x1, Pallas kernels, body(): pl.pallas_call(functools.partial(kernel, n), out_shape=jax.ShapeDtypeStru...  28.6 us
    unnamed x3, local copies, waits for them, and re-layouts  4.1 us

profile of v1, /device:TPU:25, one launch (start us, length us, event | category | flops | bytes accessed | tf_op | source)
XLA Modules:
  0.0 32.7 jit_solution(2190798349288917301)
XLA Ops:
  0.0 1.3 %copy.13.gate_values = bf16[16,2]{1,0:T(8,128)(2,1)} copy(bf16[16,2]{0,1:T(2,128)(2,1)} %param.18) | data formatting | bytes 128 | tf_op args[7]
  1.3 1.4 %copy.12.expert_ids = s32[16,2]{1,0:T(8,128)} copy(s32[16,2]{0,1:T(2,128)} %param.17) | data formatting | bytes 256 | tf_op args[6]
  2.7 28.6 %shard_map.109 = bf16[16,1536]{1,0:T(8,128)(2,1)} custom-call(s32[16]{0:T(128)} %lengths.1, bf16[16,3072]{1,0:T(8,128)(2,1)} %queries.1, bf16[16,128,512]{2,1,0:T(8,128)(2,1)} %cache_keys.1, bf16[16,128,512]{2,1,0:T(8,128)(2,1)} %cache_values.1, bf16[16,3072]{1,0:T(8,128)(2,1)} %residual_in.1, f32[1,3072]{1,0:T(1,128)} %bitcast.1, s32[16,2]{1,0:T(8,128)} %copy.12.expert_ids, ...), custom_call_target="tpu_custom_call" | custom-call | tf_op jit(solution)/shard_map/pallas_call | solution.py:235
  31.3 1.4 %copy.15 = bf16[16,1536]{1,0:T(8,128)(2,1)} copy(bf16[16,1536]{1,0:T(8,128)(2,1)} %shard_map.109) | data formatting | bytes 98304

commit v2 on v1

--- a/solution.py
+++ b/solution.py
@@ -39,22 +39,43 @@
     resid_halves,
     rows_in,
     parts,
+    partial,
+    summed,
     returned,
     load_sem,
     row_send,
     row_recv,
+    pass_send,
+    pass_recv,
     side_send,
     side_recv,
     part_send,
     part_recv,
+    sum_send,
+    sum_recv,
 ):
     me = lax.axis_index("shard")
     side = lax.axis_index("side")
     other = 1 - side
+    members = n // EXPERTS
+    team = lax.div(me, members)
+    member = lax.rem(me, members)
+    teams = []
+    for i in range(EXPERTS):
+        flipped = team
+        for bit in (1, 2):
+            if i & bit:
+                flipped = flipped + bit - 2 * bit * lax.rem(lax.div(team, bit), 2)
+        teams.append(flipped)
+
+    def after(j):
+        return lax.rem(member + j, members)
+
+    def before(j):
+        return lax.rem(member - j + members, members)
     row_count, width = residual_in.shape
     half = width // 2
     context = keys.shape[1]
-    group_size = n // EXPERTS
 
     loads = [
         pltpu.make_async_copy(cache_keys, keys, load_sem.at[0]),
@@ -71,13 +92,31 @@
     barrier = pltpu.get_barrier_semaphore()
     pl.semaphore_signal(barrier, inc=1, device_id={"side": other}, device_id_type=MESH)
 
-    def greet(k, carry):
-        pl.semaphore_signal(
-            barrier, inc=1, device_id={"shard": lax.rem(me + k, n)}, device_id_type=MESH
-        )
-        return carry
-
-    lax.fori_loop(1, n, greet, 0)
+    def greet(shard):
+        pl.semaphore_signal(barrier, inc=1, device_id={"shard": shard}, device_id_type=MESH)
+
+    def others(step):
+        def run(j, carry):
+            step(j)
+            return carry
+
+        lax.fori_loop(1, members, run, 0)
+
+    for i in range(1, EXPERTS):
+        greet(teams[i] * members + member)
+    others(lambda j: greet(team * members + after(j)))
+
+    ids = expert_ids[...]
+    gates = gate_values[...].astype(jnp.float32)
+    diagonal = lax.broadcasted_iota(jnp.int32, (row_count, row_count), 0) == (
+        lax.broadcasted_iota(jnp.int32, (row_count, row_count), 1)
+    )
+
+    def weight(expert):
+        along = jnp.sum(jnp.where(ids == expert, gates, 0.0), axis=0, keepdims=True)
+        return jnp.sum(jnp.where(diagonal, along, 0.0), axis=1, keepdims=True)
+
+    row_weights = [weight(teams[i]) for i in range(EXPERTS)]
 
     for h in range(QH):
         heads[:, h, :] = queries[:, h * HD : (h + 1) * HD].astype(jnp.float32)
@@ -119,61 +158,83 @@
         normed = (widened[h] * scale * norm_gain[:, h * HD : (h + 1) * HD]).astype(jnp.bfloat16)
         rows_in[h // (QH // 2), me, :, (h % (QH // 2)) * HD : (h % (QH // 2) + 1) * HD] = normed
 
-    pl.semaphore_wait(barrier, n)
-
-    def row_copy(k):
+    pl.semaphore_wait(barrier, EXPERTS - 1 + members)
+
+    def block_copy(block, send_sem, recv_sem, device_id):
         return pltpu.make_async_remote_copy(
-            src_ref=rows_in.at[side, me],
-            dst_ref=rows_in.at[side, me],
-            send_sem=row_send.at[k],
-            recv_sem=row_recv.at[k],
-            device_id={"shard": lax.rem(me + k, n)},
+            src_ref=rows_in.at[side, block],
+            dst_ref=rows_in.at[side, block],
+            send_sem=send_sem,
+            recv_sem=recv_sem,
+            device_id=device_id,
             device_id_type=MESH,
         )
 
-    def side_copy(k):
-        source = lax.rem(me - k + n, n)
+    def row_copy(i):
+        return block_copy(
+            me, row_send.at[i], row_recv.at[i], {"shard": teams[i] * members + member}
+        )
+
+    def pass_copy(i, j):
+        return block_copy(
+            teams[i] * members + member,
+            pass_send.at[i * members + j],
+            pass_recv.at[i * members + j],
+            {"shard": team * members + after(j)},
+        )
+
+    def side_copy(i, j):
+        return block_copy(
+            teams[i] * members + before(j),
+            side_send.at[i * members + j],
+            side_recv.at[i * members + j],
+            {"side": other},
+        )
+
+    def part_copy(i, j):
         return pltpu.make_async_remote_copy(
-            src_ref=rows_in.at[side, source],
-            dst_ref=rows_in.at[side, source],
-            send_sem=side_send.at[k],
-            recv_sem=side_recv.at[k],
-            device_id={"side": other},
+            src_ref=parts.at[teams[i] * members + after(j)],
+            dst_ref=partial.at[i * members + j],
+            send_sem=part_send.at[i * members + j],
+            recv_sem=part_recv.at[i * members + j],
+            device_id={"shard": team * members + after(j)},
             device_id_type=MESH,
         )
 
-    def part_copy(k):
-        target = lax.rem(me + k, n)
+    def sum_copy(i):
         return pltpu.make_async_remote_copy(
-            src_ref=parts.at[target],
-            dst_ref=returned.at[k],
-            send_sem=part_send.at[k],
-            recv_sem=part_recv.at[k],
-            device_id={"shard": target},
+            src_ref=summed.at[i],
+            dst_ref=returned.at[i],
+            send_sem=sum_send.at[i],
+            recv_sem=sum_recv.at[i],
+            device_id={"shard": teams[i] * members + member},
             device_id_type=MESH,
         )
 
-    def each(step):
-        def run(k, carry):
-            step(k)
-            return carry
-
-        lax.fori_loop(1, n, run, 0)
-
-    each(lambda k: row_copy(k).start())
-
-    def pass_on(k):
-        row_copy(k).wait_recv()
-        side_copy(k).start()
-
-    each(pass_on)
+    for i in range(1, EXPERTS):
+        row_copy(i).start()
+    others(lambda j: pass_copy(0, j).start())
+    for i in range(1, EXPERTS):
+        row_copy(i).wait_recv()
+        others(lambda j: pass_copy(i, j).start())
+        side_copy(i, 0).start()
+    for i in range(EXPERTS):
+
+        def swap(j):
+            pass_copy(i, j).wait_recv()
+            side_copy(i, j).start()
+
+        others(swap)
     loads[2].wait()
     loads[3].wait()
     own = rows_in[side].reshape(n * row_count, half)
     own_cols = pl.ds(pl.multiple_of(side * half, half), half)
     gate_pre = jnp.dot(own, gate_w[own_cols, :], preferred_element_type=jnp.float32)
     up_pre = jnp.dot(own, up_w[own_cols, :], preferred_element_type=jnp.float32)
-    each(lambda k: side_copy(k).wait_recv())
+    for i in range(EXPERTS):
+        if i:
+            side_copy(i, 0).wait_recv()
+        others(lambda j: side_copy(i, j).wait_recv())
     swapped = rows_in[other].reshape(n * row_count, half)
     other_cols = pl.ds(pl.multiple_of(other * half, half), half)
     gate_pre += jnp.dot(swapped, gate_w[other_cols, :], preferred_element_type=jnp.float32)
@@ -185,30 +246,41 @@
         .astype(jnp.bfloat16)
         .reshape(n, row_count, half)
     )
-    each(lambda k: part_copy(k).start())
-
-    ids = expert_ids[...]
-    gates = gate_values[...].astype(jnp.float32)
-
-    def weight(source):
-        match = ids == lax.div(source, group_size)
-        return jnp.sum(jnp.where(match, gates, 0.0), axis=-1, keepdims=True)
-
-    total = weight(me) * parts[me].astype(jnp.float32)
-
-    def gather(k, total):
-        part_copy(k).wait_recv()
-        return total + weight(lax.rem(me - k + n, n)) * returned[k].astype(jnp.float32)
-
-    total = lax.fori_loop(1, n, gather, total)
+
+    order = list(range(1, EXPERTS)) + [0]
+    for i in order:
+        others(lambda j: part_copy(i, j).start())
+
+    def team_sum(i):
+        def add(j, total):
+            part_copy(i, j).wait_recv()
+            return total + partial[i * members + j].astype(jnp.float32)
+
+        return lax.fori_loop(
+            1, members, add, parts[teams[i] * members + member].astype(jnp.float32)
+        )
+
+    for i in range(1, EXPERTS):
+        summed[i] = team_sum(i).astype(jnp.bfloat16)
+        sum_copy(i).start()
+    total = row_weights[0] * team_sum(0)
+    for i in range(1, EXPERTS):
+        sum_copy(i).wait_recv()
+        total += row_weights[i] * returned[i].astype(jnp.float32)
     out[...] = (resid_halves[side].astype(jnp.float32) + total).astype(jnp.bfloat16)
 
-    def finish(k):
-        row_copy(k).wait_send()
-        side_copy(k).wait_send()
-        part_copy(k).wait_send()
-
-    each(finish)
+    for i in range(EXPERTS):
+        if i:
+            row_copy(i).wait_send()
+            side_copy(i, 0).wait_send()
+            sum_copy(i).wait_send()
+
+        def finish(j):
+            pass_copy(i, j).wait_send()
+            side_copy(i, j).wait_send()
+            part_copy(i, j).wait_send()
+
+        others(finish)
 
 
 def body(
@@ -249,13 +321,19 @@
             pltpu.VMEM((2, n, row_count, half), jnp.bfloat16),
             pltpu.VMEM((n, row_count, half), jnp.bfloat16),
             pltpu.VMEM((n, row_count, half), jnp.bfloat16),
+            pltpu.VMEM((EXPERTS, row_count, half), jnp.bfloat16),
+            pltpu.VMEM((EXPERTS, row_count, half), jnp.bfloat16),
             dma((5,)),
-            dma((n,)),
-            dma((n,)),
-            dma((n,)),
-            dma((n,)),
-            dma((n,)),
-            dma((n,)),
+            dma((EXPERTS,)),
+            dma((EXPERTS,)),
+            dma((n,)),
+            dma((n,)),
+            dma((n,)),
+            dma((n,)),
+            dma((n,)),
+            dma((n,)),
+            dma((EXPERTS,)),
+            dma((EXPERTS,)),
         ],
         compiler_params=pltpu.CompilerParams(
             collective_id=0, has_side_effects=True, vmem_limit_bytes=56 * 1024 * 1024
@@ -267,8 +345,8 @@
         cache_values,
         residual_in,
         norm_gain.reshape(1, width),
-        expert_ids,
-        gate_values,
+        expert_ids.T,
+        gate_values.T,
         w_gate,
         w_up,
         w_down,

time: 33 us -> 30.1 us (0.912)
  the two profiles are of different devices: /device:TPU:25 before, /device:TPU:0 now
where the time goes in v2:
time: 30.1 us; the launch traced here: 29.9 us
  Pallas kernels  28.5 us (95%)
  local copies, waits for them, and re-layouts  1.42 us (5%)
    pallas_call x1, Pallas kernels, body(): pl.pallas_call(functools.partial(kernel, n), out_shape=jax.ShapeDtypeStru...  28.5 us
    unnamed x1, local copies, waits for them, and re-layouts  1.42 us

profile of v2, /device:TPU:0, one launch (start us, length us, event | category | flops | bytes accessed | tf_op | source)
XLA Modules:
  0.0 29.9 jit_solution(4932066631989937050)
XLA Ops:
  0.0 28.5 %shard_map.109 = bf16[16,1536]{1,0:T(8,128)(2,1)} custom-call(s32[16]{0:T(128)} %lengths.1, bf16[16,3072]{1,0:T(8,128)(2,1)} %queries.1, bf16[16,128,512]{2,1,0:T(8,128)(2,1)} %cache_keys.1, bf16[16,128,512]{2,1,0:T(8,128)(2,1)} %cache_values.1, bf16[16,3072]{1,0:T(8,128)(2,1)} %residual_in.1, f32[1,3072]{1,0:T(1,128)} %bitcast.3, s32[2,16]{1,0:T(2,128)} %bitcast.4, ...), custom_call_target="tpu_custom_call" | custom-call | tf_op jit(solution)/shard_map/pallas_call | solution.py:307
  28.5 1.4 %copy.13 = bf16[16,1536]{1,0:T(8,128)(2,1)} copy(bf16[16,1536]{1,0:T(8,128)(2,1)} %shard_map.109) | data formatting | bytes 98304

commit v3 on v2

--- a/solution.py
+++ b/solution.py
@@ -18,10 +18,10 @@
 def kernel(
     n,
     lengths,
-    queries,
+    queries_in,
     cache_keys,
     cache_values,
-    residual_in,
+    residual_from,
     norm_gain,
     expert_ids,
     gate_values,
@@ -29,6 +29,8 @@
     w_up,
     w_down,
     out,
+    queries,
+    residual_in,
     keys,
     values,
     gate_w,
@@ -86,8 +88,12 @@
             w_down.at[:, pl.ds(pl.multiple_of(side * half, half), half)], down_w, load_sem.at[4]
         ),
     ]
-    for load in loads:
-        load.start()
+    query_load = pltpu.make_async_copy(queries_in, queries, load_sem.at[5])
+    residual_load = pltpu.make_async_copy(residual_from, residual_in, load_sem.at[6])
+    query_load.start()
+    loads[0].start()
+    loads[1].start()
+    residual_load.start()
 
     barrier = pltpu.get_barrier_semaphore()
     pl.semaphore_signal(barrier, inc=1, device_id={"side": other}, device_id_type=MESH)
@@ -118,11 +124,14 @@
 
     row_weights = [weight(teams[i]) for i in range(EXPERTS)]
 
+    query_load.wait()
     for h in range(QH):
         heads[:, h, :] = queries[:, h * HD : (h + 1) * HD].astype(jnp.float32)
     group_of = lax.broadcasted_iota(jnp.int32, (QH, HD), 0) // (QH // KVH)
     position = lax.broadcasted_iota(jnp.int32, (QH, context), 1)
     loads[0].wait()
+    for load in loads[2:]:
+        load.start()
     probabilities = []
     for r in range(row_count):
         q = heads[r]
@@ -144,6 +153,7 @@
             picked = jnp.where(group_of == g, mixed[:, g * HD : (g + 1) * HD], picked)
         attended[r] = picked
 
+    residual_load.wait()
     squares = jnp.zeros((row_count, HD), jnp.float32)
     widened = []
     for h in range(QH):
@@ -307,9 +317,11 @@
     return pl.pallas_call(
         functools.partial(kernel, n),
         out_shape=jax.ShapeDtypeStruct((row_count, half), jnp.bfloat16),
-        in_specs=[smem, vmem, anywhere, anywhere, vmem, vmem, vmem, vmem, anywhere, anywhere, anywhere],
+        in_specs=[smem, anywhere, anywhere, anywhere, anywhere, vmem, vmem, vmem, anywhere, anywhere, anywhere],
         out_specs=vmem,
         scratch_shapes=[
+            pltpu.VMEM(queries.shape, jnp.bfloat16),
+            pltpu.VMEM(residual_in.shape, jnp.bfloat16),
             pltpu.VMEM(cache_keys.shape, jnp.bfloat16),
             pltpu.VMEM(cache_values.shape, jnp.bfloat16),
             pltpu.VMEM(w_gate.shape, jnp.bfloat16),
@@ -323,7 +335,7 @@
             pltpu.VMEM((n, row_count, half), jnp.bfloat16),
             pltpu.VMEM((EXPERTS, row_count, half), jnp.bfloat16),
             pltpu.VMEM((EXPERTS, row_count, half), jnp.bfloat16),
-            dma((5,)),
+            dma((7,)),
             dma((EXPERTS,)),
             dma((EXPERTS,)),
             dma((n,)),

time: 30.1 us -> 30.3 us (level)
  no operation moved by 1% of the time
where the time goes in v3:
time: 30.3 us; the launch traced here: 30 us
  Pallas kernels  28.6 us (94%)
  local copies, waits for them, and re-layouts  1.42 us (5%)
    pallas_call x1, Pallas kernels, body(): pl.pallas_call(functools.partial(kernel, n), out_shape=jax.ShapeDtypeStru...  28.6 us
    unnamed x1, local copies, waits for them, and re-layouts  1.42 us

profile of v3, /device:TPU:0, one launch (start us, length us, event | category | flops | bytes accessed | tf_op | source)
XLA Modules:
  0.0 30.0 jit_solution(16508853878118898056)
XLA Ops:
  0.0 28.6 %shard_map.109 = bf16[16,1536]{1,0:T(8,128)(2,1)} custom-call(s32[16]{0:T(128)} %lengths.1, bf16[16,3072]{1,0:T(8,128)(2,1)} %queries_in.1, bf16[16,128,512]{2,1,0:T(8,128)(2,1)} %cache_keys.1, bf16[16,128,512]{2,1,0:T(8,128)(2,1)} %cache_values.1, bf16[16,3072]{1,0:T(8,128)(2,1)} %residual_from.1, f32[1,3072]{1,0:T(1,128)} %bitcast.3, s32[2,16]{1,0:T(2,128)} %bitcast.4, ...), custom_call_target="tpu_custom_call" | custom-call | tf_op jit(solution)/shard_map/pallas_call | solution.py:317
  28.6 1.4 %copy.13 = bf16[16,1536]{1,0:T(8,128)(2,1)} copy(bf16[16,1536]{1,0:T(8,128)(2,1)} %shard_map.109) | data formatting | bytes 98304
